TPU v7x, 768 devices: a whole 4x8x12 slice. The times are simulated.
768 devices in a mesh: dp: 128 (over z_lo, x, y), mp: 6 (over z_hi, core).
Axes of the slice: x: 4, y: 8, z: 12 (z_hi: 3, z_lo: 4; z = z_hi * 4 + z_lo), core: 2. Of those that a mesh axis runs over, the one named last changes fastest.
Arguments:
- gradient: bfloat16 [6, 768, 24576], P('mp', 'dp'), may hold values from -90 to 90
- left_stat: float32 [6, 24576, 768], P('mp', 'dp'), may hold values from -0.2 to 2.2, as said below
- right_stat: float32 [6, 24576, 768], P('mp', 'dp'), may hold values from -0.2 to 2.2, as said below
- left_root: bfloat16 [6, 24576, 768], P('mp', 'dp'), may hold values from -0.2 to 2.2, as said below
- right_root: bfloat16 [6, 24576, 768], P('mp', 'dp'), may hold values from -0.2 to 2.2, as said below
Outputs:
- update: bfloat16 [6, 768, 24576], P('mp', 'dp')
- left_new: float32 [6, 24576, 768], P('mp', 'dp')
- right_new: float32 [6, 24576, 768], P('mp', 'dp')
Inputs may be any that keep to these rules, and one draw needn't show every extreme that they name: `left_stat`: every 768 x 768 block is symmetric. `right_stat`: every 768 x 768 block is symmetric. `left_root`: every 768 x 768 block is symmetric. `right_root`: every 768 x 768 block is symmetric.
All inputs are finite; a program needn't handle non-finite values.
Results may differ from a plain program's by a relative error of at most 0.0049.
Values may be sent and summed in bfloat16 or wider, within the bound.
A program may use at most 32 MiB of HBM per device.

v0:
```python
import jax
import jax.numpy as jnp
from jax import lax
from jax.sharding import PartitionSpec as P

BLK = 768
LANES = 4
COLS = 192


stat_decay = 0.9999
epsilon = 1e-06
clip_rms = 1.0


def swapped(value, axis, bit):
    mask = 2**bit
    pairs = [(source, source ^ mask) for source in range(lax.axis_size(axis))]
    return lax.ppermute(value, axis, pairs)


def shortened(shard):

    def short(part):
        return part.astype(jnp.bfloat16) if part.dtype == jnp.float32 else part

    return jax.tree.map(short, shard)


def butterfly(buffer, going_back):
    bit_total = lax.axis_size("dp").bit_length() - 1
    my_index = lax.axis_index("dp")
    item_count = buffer.shape[0]
    for bit_index in range(bit_total):
        upper_side = my_index >> bit_index & 1 == 1
        split_form = buffer.reshape(
            (item_count >> bit_index + 1, 2, 1 << bit_index) + buffer.shape[1:]
        )
        lower_half = split_form[:, 0]
        upper_half = split_form[:, 1]
        outgoing = jnp.where(upper_side, lower_half, upper_half)
        keep_half = jnp.where(upper_side, upper_half, lower_half)
        if going_back:
            incoming = swapped(outgoing, "dp", bit_index)
        else:
            incoming = swapped(outgoing, "dp", bit_index)
        new_lower = jnp.where(upper_side, incoming, keep_half)
        new_upper = jnp.where(upper_side, keep_half, incoming)
        buffer = jnp.stack([new_lower, new_upper], 1).reshape(buffer.shape)
    return buffer


def lane_gather(pieces, lane_index, bit_order):
    stacks = tuple((piece[None] for piece in pieces))
    for bit_index in bit_order:
        others = jax.tree.map(
            lambda part, own: part.astype(own.dtype),
            swapped(shortened(stacks), "dp", bit_index),
            stacks,
        )
        upper_half = lane_index >> bit_index & 1 == 1
        stacks = tuple(
            (
                jnp.concatenate(
                    [jnp.where(upper_half, other, current), jnp.where(upper_half, current, other)],
                    0,
                )
                for current, other in zip(stacks, others)
            )
        )
    return stacks


def on_device(gradient, left_stat, right_stat, left_root, right_root):
    bit_count = LANES.bit_length() - 1
    lane_index = lax.axis_index("dp") % LANES
    dp_count = lax.axis_size("dp")
    numel = float(dp_count * lax.axis_size("mp") * BLK * COLS)
    flat_rows = gradient[0]
    row_count = flat_rows.shape[0]
    outbound = flat_rows.reshape(row_count, dp_count, COLS).transpose(1, 0, 2)
    own_cols = butterfly(outbound, False).reshape(BLK, COLS)
    gstack, lstack = lane_gather((own_cols, left_root[0]), lane_index, list(range(bit_count)))
    lroot_full = lstack.reshape(BLK, BLK)
    rows_mine = lax.dynamic_slice_in_dim(gstack, lane_index * COLS, COLS, 1)
    left_inc = jnp.einsum("lic,ljc->ij", rows_mine, gstack, preferred_element_type=jnp.float32)
    right_inc = jnp.einsum(
        "rc,lrd->cld", own_cols, gstack, preferred_element_type=jnp.float32
    ).reshape(COLS, BLK)
    rroot_rows = right_root[0].reshape(COLS, LANES, COLS)
    mixed = jnp.einsum(
        "lrd,cld->rc", gstack, rroot_rows, preferred_element_type=jnp.float32
    ).astype(jnp.bfloat16)
    precond = jnp.dot(lroot_full, mixed, preferred_element_type=jnp.float32)
    grad_square = jnp.mean(jnp.square(gstack.astype(jnp.float32)))
    prec_total = jnp.sum(jnp.square(precond))
    for bit_index in range(bit_count):
        prec_total = prec_total + swapped(prec_total, "dp", bit_index)
    prec_square = prec_total / float(BLK * BLK)
    grafted = precond * jnp.sqrt(grad_square) * lax.rsqrt(prec_square + epsilon)
    total = lax.psum(jnp.sum(jnp.square(grafted)), ("dp", "mp")) / numel
    factor = jnp.minimum(1.0, clip_rms * lax.rsqrt(total + epsilon))
    scaled = (grafted * factor).astype(jnp.bfloat16)
    returned = butterfly(scaled.reshape(dp_count, row_count, COLS), True)
    restored = returned.transpose(1, 0, 2).reshape(row_count, dp_count * COLS)
    left_out = stat_decay * left_stat[0] + (1.0 - stat_decay) * left_inc
    right_out = stat_decay * right_stat[0] + (1.0 - stat_decay) * right_inc
    return (restored[None], left_out[None], right_out[None])


def solution(mesh):
    placed = (
        P("mp", "dp", None),
        P("mp", "dp", None),
        P("mp", "dp", None),
        P("mp", "dp", None),
        P("mp", "dp", None),
    )
    return jax.shard_map(
        on_device,
        mesh=mesh,
        in_specs=placed,
        out_specs=(P("mp", "dp", None), P("mp", "dp", None), P("mp", "dp", None)),
        check_vma=False,
    )
```

profile of v0, /device:TPU:1, one launch (start us, length us, event | category | flops | bytes accessed | tf_op | source)
XLA Modules:
  0.0 357.3 jit_solution(17109467031168344759)
XLA Ops:
  3.3 4.0 %collective-permute-start.2 = (bf16[64,1,6,192]{3,0,2,1:T(8,128)(2,1)S(1)}, bf16[64,1,6,192]{3,0,2,1:T(8,128)(2,1)S(1)}, u32[]{:S(2)}, u32[]{:S(2)}) collective-permute-start(bf16[64,1,6,192]{3,0,2,1:T(8,128)(2,1)S(1)} %bitcast.337), channel_id=1, source_target_pairs={{0,6},{6,0},{12,18},{18,12},{24,30},{30,24},{36,42},{42,36},{48,54... | collective-permute-start | bytes 442376 | tf_op jit(solution)/shard_map/ppermute | solution.py:19
  10.7 5.6 %collective-permute-start.3 = (bf16[32,2,6,192]{3,0,2,1:T(8,128)(2,1)S(1)}, bf16[32,2,6,192]{3,0,2,1:T(8,128)(2,1)S(1)}, u32[]{:S(2)}, u32[]{:S(2)}) collective-permute-start(bf16[32,2,6,192]{3,0,2,1:T(8,128)(2,1)S(1)} %select_bitcast_fusion.14), channel_id=1, source_target_pairs={{0,12},{6,18},{12,0},{18,6},{24,36},{30,42},{36,24},{42,30},{48,60... | collective-permute-start | bytes 442376 | tf_op jit(solution)/shard_map/ppermute | solution.py:19
  16.4 5.3 %collective-permute-done.3 = bf16[32,2,6,192]{3,0,2,1:T(8,128)(2,1)S(1)} collective-permute-done((bf16[32,2,6,192]{3,0,2,1:T(8,128)(2,1)S(1)}, bf16[32,2,6,192]{3,0,2,1:T(8,128)(2,1)S(1)}, u32[]{:S(2)}, u32[]{:S(2)}) %collective-permute-start.3) | collective-permute-done | bytes 147488 | tf_op jit(solution)/shard_map/ppermute | solution.py:19
  22.9 11.7 %collective-permute-start.4 = (bf16[16,4,6,192]{3,0,2,1:T(8,128)(2,1)S(1)}, bf16[16,4,6,192]{3,0,2,1:T(8,128)(2,1)S(1)}, u32[]{:S(2)}, u32[]{:S(2)}) collective-permute-start(bf16[16,4,6,192]{3,0,2,1:T(8,128)(2,1)S(1)} %select_bitcast_fusion.13), channel_id=1, source_target_pairs={{0,24},{6,30},{12,36},{18,42},{24,0},{30,6},{36,12},{42,18},{48,72... | collective-permute-start | bytes 442376 | tf_op jit(solution)/shard_map/ppermute | solution.py:19
  34.6 3.0 collective-permute-done.4
  39.1 7.6 %collective-permute-start.5 = (bf16[8,8,6,192]{3,1,2,0:T(8,128)(2,1)S(1)}, bf16[8,8,6,192]{3,1,2,0:T(8,128)(2,1)S(1)}, u32[]{:S(2)}, u32[]{:S(2)}) collective-permute-start(bf16[8,8,6,192]{3,1,2,0:T(8,128)(2,1)S(1)} %fusion.30), channel_id=1, source_target_pairs={{0,48},{6,54},{12,60},{18,66},{24,72},{30,78},{36,84},{42,90},{48,... | collective-permute-start | bytes 442376 | tf_op jit(solution)/shard_map/ppermute | solution.py:19
  50.4 5.5 %collective-permute-start.6 = (bf16[4,16,6,192]{3,1,2,0:T(8,128)(2,1)S(1)}, bf16[4,16,6,192]{3,1,2,0:T(8,128)(2,1)S(1)}, u32[]{:S(2)}, u32[]{:S(2)}) collective-permute-start(bf16[4,16,6,192]{3,1,2,0:T(8,128)(2,1)S(1)} %fusion.15), channel_id=1, source_target_pairs={{0,96},{6,102},{12,108},{18,114},{24,120},{30,126},{36,132},{42,13... | collective-permute-start | bytes 442376 | tf_op jit(solution)/shard_map/ppermute | solution.py:19
  59.1 4.2 %collective-permute-start.7 = (bf16[2,32,6,192]{3,1,2,0:T(8,128)(2,1)S(1)}, bf16[2,32,6,192]{3,1,2,0:T(8,128)(2,1)S(1)}, u32[]{:S(2)}, u32[]{:S(2)}) collective-permute-start(bf16[2,32,6,192]{3,1,2,0:T(8,128)(2,1)S(1)} %fusion.14), channel_id=1, source_target_pairs={{0,192},{6,198},{12,204},{18,210},{24,216},{30,222},{36,228},{42,2... | collective-permute-start | bytes 442376 | tf_op jit(solution)/shard_map/ppermute | solution.py:19
  63.3 3.3 collective-permute-done.7
  66.8 5.5 %collective-permute-start.8 = (bf16[1,64,6,192]{3,1,2,0:T(8,128)(2,1)S(1)}, bf16[1,64,6,192]{3,1,2,0:T(8,128)(2,1)S(1)}, u32[]{:S(2)}, u32[]{:S(2)}) collective-permute-start(bf16[1,64,6,192]{3,1,2,0:T(8,128)(2,1)S(1)} %select_bitcast_fusion.6), channel_id=1, source_target_pairs={{0,384},{6,390},{12,396},{18,402},{24,408},{30,414},{36,420},{42,4... | collective-permute-start | bytes 442376 | tf_op jit(solution)/shard_map/ppermute | solution.py:19
  74.3 3.2 collective-permute-done.8
  80.4 11.1 %collective-permute-start.1 = (bf16[2,192,768]{2,1,0:T(8,128)(2,1)S(1)}, bf16[2,192,768]{2,1,0:T(8,128)(2,1)S(1)}, u32[]{:S(2)}, u32[]{:S(2)}) collective-permute-start(bf16[2,192,768]{2,1,0:T(8,128)(2,1)S(1)} %pad_maximum_fusion.2), channel_id=1, source_target_pairs={{0,12},{6,18},{12,0},{18,6},{24,36},{30,42},{36,24},{42,30},{48,60... | collective-permute-start | bytes 1769480 | tf_op jit(solution)/shard_map/ppermute | solution.py:19
  92.4 5.6 %collective-permute-start.10 = (bf16[2,768,192]{1,2,0:T(8,128)(2,1)}, bf16[2,768,192]{1,2,0:T(8,128)(2,1)}, u32[]{:S(2)}, u32[]{:S(2)}) collective-permute-start(bf16[2,768,192]{1,2,0:T(8,128)(2,1)} %pad_maximum_fusion.3), channel_id=1, source_target_pairs={{0,12},{6,18},{12,0},{18,6},{24,36},{30,42},{36,24},{42,30},{48,60... | collective-permute-start | bytes 1769480 | tf_op jit(solution)/shard_map/ppermute | solution.py:19
  99.1 29.0 %collective-permute-done.1 = bf16[2,192,768]{2,1,0:T(8,128)(2,1)S(1)} collective-permute-done((bf16[2,192,768]{2,1,0:T(8,128)(2,1)S(1)}, bf16[2,192,768]{2,1,0:T(8,128)(2,1)S(1)}, u32[]{:S(2)}, u32[]{:S(2)}) %collective-permute-start.1) | collective-permute-done | bytes 589856 | tf_op jit(solution)/shard_map/ppermute | solution.py:19
  128.4 12.5 %collective-permute-done.10 = bf16[2,768,192]{1,2,0:T(8,128)(2,1)} collective-permute-done((bf16[2,768,192]{1,2,0:T(8,128)(2,1)}, bf16[2,768,192]{1,2,0:T(8,128)(2,1)}, u32[]{:S(2)}, u32[]{:S(2)}) %collective-permute-start.10) | collective-permute-done | bytes 589856 | tf_op jit(solution)/shard_map/ppermute | solution.py:19
  152.0 4.5 %collective-permute-start.12 = (f32[]{:T(128)}, f32[]{:T(128)}, u32[]{:S(2)}, u32[]{:S(2)}) collective-permute-start(f32[]{:T(128)} %add.28), channel_id=1, source_target_pairs={{0,12},{6,18},{12,0},{18,6},{24,36},{30,42},{36,24},{42,30},{48,60... | collective-permute-start | bytes 20 | tf_op jit(solution)/shard_map/ppermute | solution.py:19
  158.6 118.8 %psum.7 = f32[]{:T(128)} all-reduce(f32[]{:T(128)} %multiply_reduce_fusion.1), channel_id=1, replica_groups=mesh['dp'=128,'mp'=6] {'dp','mp'}, use_global_device_ids=true, to_apply=%region_3.4 | all-reduce | flops 1 | bytes 8 | tf_op jit(solution)/shard_map/psum | solution.py:101
  281.3 5.7 %collective-permute-done.13 = bf16[64,1,6,192]{3,0,2,1:T(8,128)(2,1)S(1)} collective-permute-done((bf16[64,1,6,192]{3,0,2,1:T(8,128)(2,1)S(1)}, bf16[64,1,6,192]{3,0,2,1:T(8,128)(2,1)S(1)}, u32[]{:S(2)}, u32[]{:S(2)}) %collective-permute-start.13) | collective-permute-done | bytes 147488 | tf_op jit(solution)/shard_map/ppermute | solution.py:19
  289.5 11.7 %collective-permute-done.14 = bf16[32,2,6,192]{3,0,2,1:T(8,128)(2,1)S(1)} collective-permute-done((bf16[32,2,6,192]{3,0,2,1:T(8,128)(2,1)S(1)}, bf16[32,2,6,192]{3,0,2,1:T(8,128)(2,1)S(1)}, u32[]{:S(2)}, u32[]{:S(2)}) %collective-permute-start.14) | collective-permute-done | bytes 147488 | tf_op jit(solution)/shard_map/ppermute | solution.py:19
  302.4 5.2 %collective-permute-start.15 = (bf16[16,4,6,192]{3,0,2,1:T(8,128)(2,1)S(1)}, bf16[16,4,6,192]{3,0,2,1:T(8,128)(2,1)S(1)}, u32[]{:S(2)}, u32[]{:S(2)}) collective-permute-start(bf16[16,4,6,192]{3,0,2,1:T(8,128)(2,1)S(1)} %select_bitcast_fusion.4), channel_id=1, source_target_pairs={{0,24},{6,30},{12,36},{18,42},{24,0},{30,6},{36,12},{42,18},{48,72... | collective-permute-start | bytes 442376 | tf_op jit(solution)/shard_map/ppermute | solution.py:19
  307.6 11.5 %collective-permute-done.15 = bf16[16,4,6,192]{3,0,2,1:T(8,128)(2,1)S(1)} collective-permute-done((bf16[16,4,6,192]{3,0,2,1:T(8,128)(2,1)S(1)}, bf16[16,4,6,192]{3,0,2,1:T(8,128)(2,1)S(1)}, u32[]{:S(2)}, u32[]{:S(2)}) %collective-permute-start.15) | collective-permute-done | bytes 147488 | tf_op jit(solution)/shard_map/ppermute | solution.py:19
  323.1 5.2 %collective-permute-done.16 = bf16[8,8,6,192]{3,1,2,0:T(8,128)(2,1)S(1)} collective-permute-done((bf16[8,8,6,192]{3,1,2,0:T(8,128)(2,1)S(1)}, bf16[8,8,6,192]{3,1,2,0:T(8,128)(2,1)S(1)}, u32[]{:S(2)}, u32[]{:S(2)}) %collective-permute-start.16) | collective-permute-done | bytes 147488 | tf_op jit(solution)/shard_map/ppermute | solution.py:19
  331.7 5.5 %collective-permute-done.17 = bf16[4,16,6,192]{3,1,2,0:T(8,128)(2,1)S(1)} collective-permute-done((bf16[4,16,6,192]{3,1,2,0:T(8,128)(2,1)S(1)}, bf16[4,16,6,192]{3,1,2,0:T(8,128)(2,1)S(1)}, u32[]{:S(2)}, u32[]{:S(2)}) %collective-permute-start.17) | collective-permute-done | bytes 147488 | tf_op jit(solution)/shard_map/ppermute | solution.py:19
  347.4 8.5 %collective-permute-done.19 = bf16[1,64,6,192]{3,1,2,0:T(8,128)(2,1)S(1)} collective-permute-done((bf16[1,64,6,192]{3,1,2,0:T(8,128)(2,1)S(1)}, bf16[1,64,6,192]{3,1,2,0:T(8,128)(2,1)S(1)}, u32[]{:S(2)}, u32[]{:S(2)}) %collective-permute-start.19) | collective-permute-done | bytes 147488 | tf_op jit(solution)/shard_map/ppermute | solution.py:19
  (119 shorter events, 58.8 us)
Async XLA Ops:
  3.3 7.1 %collective-permute-start.2 = (bf16[64,1,6,192]{3,0,2,1:T(8,128)(2,1)S(1)}, bf16[64,1,6,192]{3,0,2,1:T(8,128)(2,1)S(1)}, u32[]{:S(2)}, u32[]{:S(2)}) collective-permute-start(bf16[64,1,6,192]{3,0,2,1:T(8,128)(2,1)S(1)} %bitcast.337), channel_id=1, source_target_pairs={{0,6},{6,0},{12,18},{18,12},{24,30},{30,24},{36,42},{42,36},{48,54... | collective-permute-start | bytes 442376 | tf_op jit(solution)/shard_map/ppermute | solution.py:19
  10.7 10.9 %collective-permute-start.3 = (bf16[32,2,6,192]{3,0,2,1:T(8,128)(2,1)S(1)}, bf16[32,2,6,192]{3,0,2,1:T(8,128)(2,1)S(1)}, u32[]{:S(2)}, u32[]{:S(2)}) collective-permute-start(bf16[32,2,6,192]{3,0,2,1:T(8,128)(2,1)S(1)} %select_bitcast_fusion.14), channel_id=1, source_target_pairs={{0,12},{6,18},{12,0},{18,6},{24,36},{30,42},{36,24},{42,30},{48,60... | collective-permute-start | bytes 442376 | tf_op jit(solution)/shard_map/ppermute | solution.py:19
  22.9 14.7 %collective-permute-start.4 = (bf16[16,4,6,192]{3,0,2,1:T(8,128)(2,1)S(1)}, bf16[16,4,6,192]{3,0,2,1:T(8,128)(2,1)S(1)}, u32[]{:S(2)}, u32[]{:S(2)}) collective-permute-start(bf16[16,4,6,192]{3,0,2,1:T(8,128)(2,1)S(1)} %select_bitcast_fusion.13), channel_id=1, source_target_pairs={{0,24},{6,30},{12,36},{18,42},{24,0},{30,6},{36,12},{42,18},{48,72... | collective-permute-start | bytes 442376 | tf_op jit(solution)/shard_map/ppermute | solution.py:19
  39.1 10.6 %collective-permute-start.5 = (bf16[8,8,6,192]{3,1,2,0:T(8,128)(2,1)S(1)}, bf16[8,8,6,192]{3,1,2,0:T(8,128)(2,1)S(1)}, u32[]{:S(2)}, u32[]{:S(2)}) collective-permute-start(bf16[8,8,6,192]{3,1,2,0:T(8,128)(2,1)S(1)} %fusion.30), channel_id=1, source_target_pairs={{0,48},{6,54},{12,60},{18,66},{24,72},{30,78},{36,84},{42,90},{48,... | collective-permute-start | bytes 442376 | tf_op jit(solution)/shard_map/ppermute | solution.py:19
  50.4 8.5 %collective-permute-start.6 = (bf16[4,16,6,192]{3,1,2,0:T(8,128)(2,1)S(1)}, bf16[4,16,6,192]{3,1,2,0:T(8,128)(2,1)S(1)}, u32[]{:S(2)}, u32[]{:S(2)}) collective-permute-start(bf16[4,16,6,192]{3,1,2,0:T(8,128)(2,1)S(1)} %fusion.15), channel_id=1, source_target_pairs={{0,96},{6,102},{12,108},{18,114},{24,120},{30,126},{36,132},{42,13... | collective-permute-start | bytes 442376 | tf_op jit(solution)/shard_map/ppermute | solution.py:19
  59.1 7.5 %collective-permute-start.7 = (bf16[2,32,6,192]{3,1,2,0:T(8,128)(2,1)S(1)}, bf16[2,32,6,192]{3,1,2,0:T(8,128)(2,1)S(1)}, u32[]{:S(2)}, u32[]{:S(2)}) collective-permute-start(bf16[2,32,6,192]{3,1,2,0:T(8,128)(2,1)S(1)} %fusion.14), channel_id=1, source_target_pairs={{0,192},{6,198},{12,204},{18,210},{24,216},{30,222},{36,228},{42,2... | collective-permute-start | bytes 442376 | tf_op jit(solution)/shard_map/ppermute | solution.py:19
  66.6 5.7 %copy-start.2 = (bf16[1,192,768]{2,1,0:T(8,128)(2,1)S(1)}, bf16[1,192,768]{2,1,0:T(8,128)(2,1)}, u32[]{:S(2)}) copy-start(bf16[1,192,768]{2,1,0:T(8,128)(2,1)} %param.8) | copy-start | bytes 884740
  66.8 10.8 %collective-permute-start.8 = (bf16[1,64,6,192]{3,1,2,0:T(8,128)(2,1)S(1)}, bf16[1,64,6,192]{3,1,2,0:T(8,128)(2,1)S(1)}, u32[]{:S(2)}, u32[]{:S(2)}) collective-permute-start(bf16[1,64,6,192]{3,1,2,0:T(8,128)(2,1)S(1)} %select_bitcast_fusion.6), channel_id=1, source_target_pairs={{0,384},{6,390},{12,396},{18,402},{24,408},{30,414},{36,420},{42,4... | collective-permute-start | bytes 442376 | tf_op jit(solution)/shard_map/ppermute | solution.py:19
  72.4 7.9 %collective-permute-start = (bf16[1,192,768]{2,1,0:T(8,128)(2,1)S(1)}, bf16[1,192,768]{2,1,0:T(8,128)(2,1)S(1)}, u32[]{:S(2)}, u32[]{:S(2)}) collective-permute-start(bf16[1,192,768]{2,1,0:T(8,128)(2,1)S(1)} %copy-done.2), channel_id=1, source_target_pairs={{0,6},{6,0},{12,18},{18,12},{24,30},{30,24},{36,42},{42,36},{48,54... | collective-permute-start | bytes 884744 | tf_op jit(solution)/shard_map/ppermute | solution.py:19
  78.3 13.2 %collective-permute-start.9 = (bf16[1,768,192]{1,2,0:T(8,128)(2,1)S(1)}, bf16[1,768,192]{1,2,0:T(8,128)(2,1)S(1)}, u32[]{:S(2)}, u32[]{:S(2)}) collective-permute-start(bf16[1,768,192]{1,2,0:T(8,128)(2,1)S(1)} %copy.177), channel_id=1, source_target_pairs={{0,6},{6,0},{12,18},{18,12},{24,30},{30,24},{36,42},{42,36},{48,54... | collective-permute-start | bytes 884744 | tf_op jit(solution)/shard_map/ppermute | solution.py:19
  80.4 17.6 %copy-start.3 = (bf16[1,192,768]{2,1,0:T(8,128)(2,1)S(1)}, bf16[1,192,768]{2,1,0:T(8,128)(2,1)}, u32[]{:S(2)}) copy-start(bf16[1,192,768]{2,1,0:T(8,128)(2,1)} %param.9) | copy-start | bytes 884740
  80.4 47.8 %collective-permute-start.1 = (bf16[2,192,768]{2,1,0:T(8,128)(2,1)S(1)}, bf16[2,192,768]{2,1,0:T(8,128)(2,1)S(1)}, u32[]{:S(2)}, u32[]{:S(2)}) collective-permute-start(bf16[2,192,768]{2,1,0:T(8,128)(2,1)S(1)} %pad_maximum_fusion.2), channel_id=1, source_target_pairs={{0,12},{6,18},{12,0},{18,6},{24,36},{30,42},{36,24},{42,30},{48,60... | collective-permute-start | bytes 1769480 | tf_op jit(solution)/shard_map/ppermute | solution.py:19
  92.4 48.5 %collective-permute-start.10 = (bf16[2,768,192]{1,2,0:T(8,128)(2,1)}, bf16[2,768,192]{1,2,0:T(8,128)(2,1)}, u32[]{:S(2)}, u32[]{:S(2)}) collective-permute-start(bf16[2,768,192]{1,2,0:T(8,128)(2,1)} %pad_maximum_fusion.3), channel_id=1, source_target_pairs={{0,12},{6,18},{12,0},{18,6},{24,36},{30,42},{36,24},{42,30},{48,60... | collective-permute-start | bytes 1769480 | tf_op jit(solution)/shard_map/ppermute | solution.py:19
  146.5 4.4 %collective-permute-start.11 = (f32[]{:T(128)}, f32[]{:T(128)}, u32[]{:S(2)}, u32[]{:S(2)}) collective-permute-start(f32[]{:T(128)} %get-tuple-element.53), channel_id=1, source_target_pairs={{0,6},{6,0},{12,18},{18,12},{24,30},{30,24},{36,42},{42,36},{48,54... | collective-permute-start | bytes 20 | tf_op jit(solution)/shard_map/ppermute | solution.py:19
  152.0 5.1 %collective-permute-start.12 = (f32[]{:T(128)}, f32[]{:T(128)}, u32[]{:S(2)}, u32[]{:S(2)}) collective-permute-start(f32[]{:T(128)} %add.28), channel_id=1, source_target_pairs={{0,12},{6,18},{12,0},{18,6},{24,36},{30,42},{36,24},{42,30},{48,60... | collective-permute-start | bytes 20 | tf_op jit(solution)/shard_map/ppermute | solution.py:19
  279.4 7.7 %collective-permute-start.13 = (bf16[64,1,6,192]{3,0,2,1:T(8,128)(2,1)S(1)}, bf16[64,1,6,192]{3,0,2,1:T(8,128)(2,1)S(1)}, u32[]{:S(2)}, u32[]{:S(2)}) collective-permute-start(bf16[64,1,6,192]{3,0,2,1:T(8,128)(2,1)S(1)} %bitcast.338), channel_id=1, source_target_pairs={{0,6},{6,0},{12,18},{18,12},{24,30},{30,24},{36,42},{42,36},{48,54... | collective-permute-start | bytes 442376 | tf_op jit(solution)/shard_map/ppermute | solution.py:19
  287.4 13.8 %collective-permute-start.14 = (bf16[32,2,6,192]{3,0,2,1:T(8,128)(2,1)S(1)}, bf16[32,2,6,192]{3,0,2,1:T(8,128)(2,1)S(1)}, u32[]{:S(2)}, u32[]{:S(2)}) collective-permute-start(bf16[32,2,6,192]{3,0,2,1:T(8,128)(2,1)S(1)} %select_bitcast_fusion.5), channel_id=1, source_target_pairs={{0,12},{6,18},{12,0},{18,6},{24,36},{30,42},{36,24},{42,30},{48,60... | collective-permute-start | bytes 442376 | tf_op jit(solution)/shard_map/ppermute | solution.py:19
  302.4 16.7 %collective-permute-start.15 = (bf16[16,4,6,192]{3,0,2,1:T(8,128)(2,1)S(1)}, bf16[16,4,6,192]{3,0,2,1:T(8,128)(2,1)S(1)}, u32[]{:S(2)}, u32[]{:S(2)}) collective-permute-start(bf16[16,4,6,192]{3,0,2,1:T(8,128)(2,1)S(1)} %select_bitcast_fusion.4), channel_id=1, source_target_pairs={{0,24},{6,30},{12,36},{18,42},{24,0},{30,6},{36,12},{42,18},{48,72... | collective-permute-start | bytes 442376 | tf_op jit(solution)/shard_map/ppermute | solution.py:19
  320.6 7.7 %collective-permute-start.16 = (bf16[8,8,6,192]{3,1,2,0:T(8,128)(2,1)S(1)}, bf16[8,8,6,192]{3,1,2,0:T(8,128)(2,1)S(1)}, u32[]{:S(2)}, u32[]{:S(2)}) collective-permute-start(bf16[8,8,6,192]{3,1,2,0:T(8,128)(2,1)S(1)} %select_bitcast_fusion.3), channel_id=1, source_target_pairs={{0,48},{6,54},{12,60},{18,66},{24,72},{30,78},{36,84},{42,90},{48,... | collective-permute-start | bytes 442376 | tf_op jit(solution)/shard_map/ppermute | solution.py:19
  328.9 8.3 %collective-permute-start.17 = (bf16[4,16,6,192]{3,1,2,0:T(8,128)(2,1)S(1)}, bf16[4,16,6,192]{3,1,2,0:T(8,128)(2,1)S(1)}, u32[]{:S(2)}, u32[]{:S(2)}) collective-permute-start(bf16[4,16,6,192]{3,1,2,0:T(8,128)(2,1)S(1)} %select_bitcast_fusion.2), channel_id=1, source_target_pairs={{0,96},{6,102},{12,108},{18,114},{24,120},{30,126},{36,132},{42,13... | collective-permute-start | bytes 442376 | tf_op jit(solution)/shard_map/ppermute | solution.py:19
  337.2 2.1 copy-start
  337.4 6.4 %collective-permute-start.18 = (bf16[2,32,6,192]{3,1,2,0:T(8,128)(2,1)S(1)}, bf16[2,32,6,192]{3,1,2,0:T(8,128)(2,1)S(1)}, u32[]{:S(2)}, u32[]{:S(2)}) collective-permute-start(bf16[2,32,6,192]{3,1,2,0:T(8,128)(2,1)S(1)} %select_bitcast_fusion.1), channel_id=1, source_target_pairs={{0,192},{6,198},{12,204},{18,210},{24,216},{30,222},{36,228},{42,2... | collective-permute-start | bytes 442376 | tf_op jit(solution)/shard_map/ppermute | solution.py:19
  343.8 2.2 copy-start.1
  344.0 11.9 %collective-permute-start.19 = (bf16[1,64,6,192]{3,1,2,0:T(8,128)(2,1)S(1)}, bf16[1,64,6,192]{3,1,2,0:T(8,128)(2,1)S(1)}, u32[]{:S(2)}, u32[]{:S(2)}) collective-permute-start(bf16[1,64,6,192]{3,1,2,0:T(8,128)(2,1)S(1)} %select_bitcast_fusion), channel_id=1, source_target_pairs={{0,384},{6,390},{12,396},{18,402},{24,408},{30,414},{36,420},{42,4... | collective-permute-start | bytes 442376 | tf_op jit(solution)/shard_map/ppermute | solution.py:19
where the time goes:
time: 358 us; the launch traced here: 357 us
  waiting for transfers between devices  119 us (33%)
  blocking collectives  119 us (33%)
  starting transfers between devices  89.4 us (25%)
  local copies, waits for them, and re-layouts  9.99 us (3%)
  other arithmetic  9.69 us (3%)
  matrix products  5.37 us (2%)
  between operations  4.72 us (1%)
    ppermute x20, waiting for transfers between devices, swapped(): return lax.ppermute(value, axis, pairs)  119 us
    psum x1, blocking collectives, on_device(): total = lax.psum(jnp.sum(jnp.square(grafted)), ('dp', 'mp')) / numel  119 us
    ppermute x20, starting transfers between devices, swapped(): return lax.ppermute(value, axis, pairs)  89.4 us
  transfers between devices with their start and end apart: 20, of which 18 were waited for; matrix products, arithmetic and copies ran while one was open for 2% of the time, Pallas kernels for 0%

commit v1 on v0

v1 whole, which is shorter than its diff:
```python
import functools

import jax
import jax.numpy as jnp
from jax import lax
from jax.experimental import pallas as pl
from jax.experimental.pallas import tpu as pltpu
from jax.sharding import PartitionSpec as P

MESH = pl.DeviceIdType.MESH
F32 = jnp.float32
BF16 = jnp.bfloat16

BLK = 768
PLANE = 16
RING = 8
SLABS = 6
ROWS = 6
QUART = 192
WIDE = 640
SUBS = 2
CHUNK = PLANE * ROWS
PART = BLK // SUBS

stat_decay = 0.9999
epsilon = 1e-06
clip_rms = 1.0


def iota(shape, dim):
    return lax.broadcasted_iota(jnp.int32, shape, dim)


def by6(v):
    q = (v * 10923) >> 16
    return q, v - q * 6


def one_hot(rows, cols, target):
    return jnp.where(iota((rows, cols), 0) == target(iota((rows, cols), 1)), 1.0, 0.0).astype(BF16)


def dot(a, b):
    return jnp.dot(a, b, preferred_element_type=F32)


def dot_nt(a, b):
    return lax.dot_general(a, b, (((1,), (1,)), ((), ())), preferred_element_type=F32)


def kernel(
    grad, lstat, rstat, lroot, rroot, upd_out, lnew_out, rnew_out,
    upd, lnew, rnew, gin, lold, rold, gsend, recv1, gfull, obuf, tbuf, rrp, lrp, order, cols, leftp, leftq, mixed, gsq, gtrue, ubuf, recvu,
    stat, recvs, msg, recvp, tot, recvt, coef, send2, recv2,
    sload, sstore, s1, r1, sx, rx, sr, rr, sl, rl, st, rt, su, ru, ss, rs, sp, rp, sm, rm, s2, r2,
):
    me = lax.axis_index("dp")
    mp = lax.axis_index("mp")
    p = me // RING
    y = me % RING
    lane = y % 4
    half = y // 4
    parity = y % 2
    upper = lane // 2

    def plane_id(off):
        t = (p + off) % PLANE
        return t, (t * RING + y, mp)

    def ring_id(off):
        t = (y + off) % RING
        return t, (p * RING + t, mp)

    def mp_id(off):
        return (me, (mp + off) % SLABS)

    def remote(src, dst, send, recv, where):
        return pltpu.make_async_remote_copy(
            src_ref=src, dst_ref=dst, send_sem=send, recv_sem=recv, device_id=where, device_id_type=MESH
        )

    loads = [
        pltpu.make_async_copy(src, dst, sload.at[i])
        for i, (src, dst) in enumerate(
            ((grad, gin), (rroot, rrp.at[parity]), (lroot, lrp.at[upper]), (lstat, lold), (rstat, rold))
        )
    ]
    loads[0].start()
    barrier = pltpu.get_barrier_semaphore()
    peers = [plane_id(o)[1] for o in range(1, PLANE)]
    peers += [ring_id(o)[1] for o in range(1, RING)]
    peers += [mp_id(o) for o in range(1, SLABS)]
    for where in peers:
        pl.semaphore_signal(barrier, inc=1, device_id=where, device_id_type=MESH)

    for cp in loads[1:]:
        cp.start()
    gsend[...] = jnp.zeros_like(gsend)
    pl.semaphore_wait(barrier, len(peers))

    def outside(q):
        return (q * QUART + 127) // 128

    def lanes128(k):
        return pl.ds(pl.multiple_of(k * 128, 128), 128)

    def root_copies(kind, src, dst, slot, shift):
        copies = []
        for i in range(1, 6):
            part = lanes128((outside(lane + shift) + i) % 6)
            cp = remote(
                src.at[:, part], dst.at[slot, :, part], sx.at[kind, i], rx.at[kind, i], (me + shift, mp)
            )
            cp.start()
            copies.append(cp)
        return copies

    shift_r, shift_l = 1 - 2 * parity, 2 - 4 * upper
    xr = root_copies(0, rroot, rrp, parity, shift_r)
    xl = root_copies(1, lroot, lrp, upper, shift_l)

    def fill(ref, slot, shift):
        own = outside(lane)
        pick = jnp.where(iota((QUART, BLK), 1) == iota((QUART, BLK), 0) + (lane + shift) * QUART, 1.0, 0.0)
        mine = ref[slot, pl.ds(pl.multiple_of(own * 128 - lane * QUART, 64), 128), :]
        ref[1 - slot, :, lanes128(own)] = dot_nt(pick.astype(BF16), mine).astype(BF16)

    loads[0].wait()
    first = []
    for sub in range(SUBS):
        for q in range(PLANE):
            for h in range(2):
                c = (2 * q + h) * BLK + sub * PART
                gsend[sub, q, 8 * h : 8 * h + ROWS, :] = gin[:, c : c + PART]
        copies = []
        for off in range(1, PLANE):
            t, where = plane_id(off)
            cp = remote(gsend.at[sub, t], recv1.at[sub, p], s1.at[sub, off], r1.at[sub, off], where)
            cp.start()
            copies.append(cp)
        first.append(copies)
        recv1[sub, p] = gsend[sub, p]

    def compact(c):
        i = c & 7
        h = (c >> 3) & 1
        row = jnp.where(h == half, 0, CHUNK) + (c >> 4) * ROWS + i
        return jnp.where(i < ROWS, row, -1)

    def ordered(c):
        q = c >> 5
        yy = (q * 21846) >> 16
        pp, i = by6(c - yy * CHUNK)
        return pp * (RING * ROWS) + yy * ROWS + i

    def by_ring(c):
        s = (c >= QUART).astype(jnp.int32)
        q = ((c >> 4) * 21846) >> 16
        xx = q - 4 * s
        yy, i = by6(c - q * 48)
        return yy * 48 + s * 24 + xx * ROWS + i

    def spread(c):
        h = (c >= 48).astype(jnp.int32)
        q, i = by6(c - 48 * h)
        return q * 16 + h * ROWS + i

    def spread_last(block):
        def row(c):
            h = (c >= 48).astype(jnp.int32)
            q, i = by6(c - 48 * h)
            low = (i >= 3).astype(jnp.int32)
            return jnp.where(i - 3 * low == block, q * 16 + 12 + 2 * h + low, -1)

        return row

    order[...] = one_hot(BLK, BLK, ordered)
    compactor = one_hot(2 * CHUNK, PLANE * 16, compact)
    def hop(way, dist, sub, src):
        step = 1 if way == 0 else RING - 1
        slot = (y + (RING - step) * dist) % RING
        send, recv = (sr, rr) if way == 0 else (sl, rl)
        where = ring_id(step)[1]
        dst = gfull.at[sub, slot]
        return remote(dst if src is None else src, dst, send.at[dist, sub], recv.at[dist + 1, sub], where)

    def transit(way, sub):
        step = 1 if way == 0 else RING - 1
        return remote(
            obuf.at[sub], tbuf.at[way, sub], st.at[way, sub], rt.at[way, sub], ring_id(step)[1]
        )

    def slot_of(way, dist):
        return (y + (RING - 1 if way == 0 else 1) * dist) % RING

    def arrival(way, dist, sub):
        recv = rr if way == 0 else rl
        slot = slot_of(way, dist)
        where = ring_id(1 if way == 0 else RING - 1)[1]
        there = gfull.at[sub, slot]
        remote(there, there, recv.at[dist, sub], recv.at[dist, sub], where).wait_recv()

    def multiply(slot):
        total, squares = 0.0, 0.0
        for sub in range(SUBS):
            chunk = gfull[sub, slot]
            total = total + dot(chunk, cols[PART * sub : PART * sub + PART])
            squares = squares + jnp.sum(jnp.square(chunk.astype(F32)), keepdims=True)
        mixed[slot] = total.astype(BF16)
        gsq[slot] = jnp.broadcast_to(squares, (8, 128))

    ranks = (lane, 3 - lane)
    for sub in range(SUBS):
        for cp in first[sub]:
            cp.wait_recv()
        packed = dot(compactor, recv1[sub].reshape(PLANE * 16, PART)).astype(BF16)
        gfull[sub, y] = packed[:CHUNK]
        obuf[sub] = packed[CHUNK:]
        for way in range(2):

            @pl.when(ranks[way] == 2)
            def _():
                transit(way, sub).start()

        for way in range(2):

            @pl.when(ranks[way] <= 2)
            def _():
                hop(way, 0, sub, None).start()

            @pl.when(ranks[way] == 3)
            def _():
                hop(way, 0, sub, obuf.at[sub]).start()

    for dist in range(1, 6):
        for sub in range(SUBS):
            for way in range(2):
                rank = ranks[way]
                if dist == 1:

                    @pl.when(rank == 3)
                    def _():
                        transit(way, sub).wait_recv()
                        hop(way, 1, sub, tbuf.at[way, sub]).start()

                @pl.when(dist <= rank + 2)
                def _():
                    arrival(way, dist, sub)
                    if dist <= 4:

                        @pl.when(rank <= 2)
                        def _():
                            hop(way, dist, sub, None).start()

        if dist == 3:
            loads[1].wait()
            loads[2].wait()
            for cp in xr:
                cp.wait_recv()
            fill(rrp, parity, shift_r)
            cols[...] = jnp.transpose(rrp[...].reshape(384, BLK))
            for cp in xl:
                cp.wait_recv()
            fill(lrp, upper, shift_l)
            left_rows = dot(one_hot(384, 384, by_ring), lrp[...].reshape(384, BLK)).astype(BF16)
            leftp[...] = left_rows
        if dist < 4:
            continue
        if dist == 4:
            leftq[...] = dot(leftp[...], order[...]).astype(BF16)
            multiply(y)
        for back in (1, 2, 3, 4) if dist == 4 else (dist,):
            for way in range(2):

                @pl.when(back <= ranks[way] + 2)
                def _():
                    multiply(slot_of(way, back))

    direction = dot(leftq[...], mixed[...].reshape(BLK, 384))
    partial = jnp.sum(jnp.square(direction), keepdims=True)
    stat[...] = jnp.where(iota((8, 128), 0) == 0, partial, jnp.sum(gsq[...], axis=0) * 0.25)
    ring_s = []
    for off in range(1, RING):
        t, where = ring_id(off)
        cs = remote(stat, recvs.at[y], ss.at[off], rs.at[off], where)
        cs.start()
        ring_s.append(cs)
    ubuf[...] = direction.astype(BF16).reshape(RING, 48, 384)
    ring_u = []
    for off in (4, 3, 5, 2, 6, 1, 7):
        t, where = ring_id(off)
        cu = remote(ubuf.at[t], recvu.at[y], su.at[off], ru.at[off], where)
        cu.start()
        ring_u.append(cu)
    recvs[y] = stat[...]
    recvu[y] = ubuf[y]

    def reorder(k):
        for sub in range(SUBS):
            gtrue[QUART * k : QUART * k + QUART, PART * sub : PART * sub + PART] = dot(
                order[QUART * k : QUART * k + QUART], gfull[sub].reshape(BLK, PART)
            ).astype(BF16)

    reorder(0)
    reorder(1)

    for cs in ring_s:
        cs.wait_recv()
    for h in range(2):
        msg[h] = recvs[4 * h] + recvs[4 * h + 1] + recvs[4 * h + 2] + recvs[4 * h + 3]
    plane_s = []
    for off in range(1, PLANE):
        t, where = plane_id(off)
        cp = remote(msg, recvp.at[p], sp.at[off], rp.at[off], where)
        cp.start()
        plane_s.append(cp)
    recvp[p] = msg[...]
    reorder(2)
    reorder(3)

    loads[3].wait()
    loads[4].wait()
    rows = gtrue[pl.ds(pl.multiple_of(lane * QUART, QUART), QUART), :]
    lnew[...] = stat_decay * lold[...] + (1.0 - stat_decay) * dot_nt(rows, gtrue[...])
    stores = [pltpu.make_async_copy(lnew, lnew_out, sstore.at[0])]
    stores[0].start()
    pick = jnp.where(iota((QUART, BLK), 1) == iota((QUART, BLK), 0) + lane * QUART, 1.0, 0.0).astype(BF16)
    columns = dot_nt(pick, gtrue[...]).astype(BF16)
    rnew[...] = stat_decay * rold[...] + (1.0 - stat_decay) * dot(columns, gtrue[...])
    stores.append(pltpu.make_async_copy(rnew, rnew_out, sstore.at[1]))
    stores[1].start()

    for cp in first[0] + first[1] + xr + xl:
        cp.wait_send()
    for way in range(2):
        rank = ranks[way]

        @pl.when(rank == 2)
        def _():
            for sub in range(SUBS):
                transit(way, sub).wait_send()

        for dist in range(5):
            count = jnp.where(rank == 3, 2, rank + 3)

            @pl.when(dist < count)
            def _():
                for sub in range(SUBS):
                    hop(way, dist, sub, None).wait_send()

    place = one_hot(128, 96, spread)
    place_last = [one_hot(128, 96, spread_last(block)) for block in range(3)]
    for cu in ring_u:
        cu.wait_recv()
    for e in range(2):
        both = [jnp.concatenate([recvu[2 * k + e], recvu[4 + 2 * k + e]], axis=0) for k in range(2)]
        both = jnp.concatenate(both, axis=1)
        last = jnp.concatenate([dot(at, both[:, WIDE:]) for at in place_last], axis=1)
        out = dot(place, both[:, :WIDE])
        out = jnp.concatenate([out[:, :384] + last, out[:, 384:]], axis=1).astype(BF16)
        for s in range(2):
            for xx in range(4):
                send2[(e + 2 * s) * 4 + xx] = out[(4 * s + xx) * 16 : (4 * s + xx) * 16 + 16]
    second = []
    for off in range(1, PLANE):
        t, where = plane_id(off)
        cp = remote(send2.at[t], recv2.at[p], s2.at[off], r2.at[off], where)
        cp.start()
        second.append(cp)

    for cp in plane_s:
        cp.wait_recv()
    size = float(BLK * BLK)
    square = recvp[:, :, 0:1, :] * (1.0 / size)
    gmean = recvp[:, :, 1:2, :] * (1.0 / size)
    root = lax.rsqrt(square + epsilon)
    slab = jnp.sum(gmean * square * root * root, axis=(0, 1))
    tot[...] = jnp.broadcast_to(slab, (8, 128))
    mp_s = []
    for off in range(1, SLABS):
        cp = remote(tot, recvt.at[mp], sm.at[off], rm.at[off], mp_id(off))
        cp.start()
        mp_s.append(cp)
    recvt[mp] = tot[...]
    recv2[p] = send2[p]

    for cp in ring_s + ring_u + plane_s:
        cp.wait_send()
    for cp in mp_s:
        cp.wait_recv()
    total = jnp.sum(recvt[...], axis=0)[0:1] * (1.0 / float(2 * PLANE * SLABS))
    factor = jnp.minimum(1.0, clip_rms * lax.rsqrt(total + epsilon))
    coef[...] = jnp.sqrt(gmean) * root * factor[None, None]

    def finish(q):
        got = recv2[q].astype(F32)
        for h in range(2):
            c = pl.multiple_of((2 * q + h) * BLK, 128)
            scale = coef[q, h][:, 0:1]
            upd[:, pl.ds(c, WIDE)] = (got[ROWS * h : ROWS * h + ROWS] * scale).astype(BF16)
            last = [got[12 + 2 * h + r : 13 + 2 * h + r, 128 * k : 128 * k + 128] for r in range(2) for k in range(3)]
            upd[:, pl.ds(c + WIDE, 128)] = (jnp.concatenate(last, axis=0) * scale).astype(BF16)

    finish(p)
    for off in range(1, PLANE):
        second[off - 1].wait_recv()
        finish((p + PLANE - off) % PLANE)
    stores.append(pltpu.make_async_copy(upd, upd_out, sstore.at[2]))
    stores[2].start()

    for cp in second + mp_s:
        cp.wait_send()
    for cp in stores:
        cp.wait()


def place_out(upd, lnew, rnew, upd_out, lnew_out, rnew_out, upd_mid, lnew_mid, rnew_mid, sem):
    legs = ((lnew, lnew_mid, lnew_out), (rnew, rnew_mid, rnew_out), (upd, upd_mid, upd_out))
    inward = [pltpu.make_async_copy(a, b, sem.at[0, i]) for i, (a, b, _) in enumerate(legs)]
    outward = [pltpu.make_async_copy(b, c, sem.at[1, i]) for i, (_, b, c) in enumerate(legs)]
    for cp in inward:
        cp.start()
    for there, on in zip(inward, outward):
        there.wait()
        on.start()
    for cp in outward:
        cp.wait()


def on_device(gradient, left_stat, right_stat, left_root, right_root):
    hbm = pl.BlockSpec(memory_space=pltpu.HBM)
    dma = pltpu.SemaphoreType.DMA
    shapes = (
        jax.ShapeDtypeStruct((ROWS, 2 * PLANE * BLK), BF16),
        jax.ShapeDtypeStruct((QUART, BLK), F32),
        jax.ShapeDtypeStruct((QUART, BLK), F32),
    )
    update, left_new, right_new = pl.pallas_call(
        kernel,
        out_shape=shapes,
        in_specs=[hbm] * 5,
        out_specs=(hbm, hbm, hbm),
        scratch_shapes=[
            pltpu.VMEM((ROWS, 2 * PLANE * BLK), BF16),
            pltpu.VMEM((QUART, BLK), F32),
            pltpu.VMEM((QUART, BLK), F32),
            pltpu.VMEM((ROWS, 2 * PLANE * BLK), BF16),
            pltpu.VMEM((QUART, BLK), F32),
            pltpu.VMEM((QUART, BLK), F32),
            pltpu.VMEM((SUBS, PLANE, 16, PART), BF16),
            pltpu.VMEM((SUBS, PLANE, 16, PART), BF16),
            pltpu.VMEM((SUBS, RING, CHUNK, PART), BF16),
            pltpu.VMEM((SUBS, CHUNK, PART), BF16),
            pltpu.VMEM((2, SUBS, CHUNK, PART), BF16),
            pltpu.VMEM((2, QUART, BLK), BF16),
            pltpu.VMEM((2, QUART, BLK), BF16),
            pltpu.VMEM((BLK, BLK), BF16),
            pltpu.VMEM((BLK, 384), BF16),
            pltpu.VMEM((384, BLK), BF16),
            pltpu.VMEM((384, BLK), BF16),
            pltpu.VMEM((RING, CHUNK, 384), BF16),
            pltpu.VMEM((RING, 8, 128), F32),
            pltpu.VMEM((BLK, BLK), BF16),
            pltpu.VMEM((RING, 48, 384), BF16),
            pltpu.VMEM((RING, 48, 384), BF16),
            pltpu.VMEM((8, 128), F32),
            pltpu.VMEM((RING, 8, 128), F32),
            pltpu.VMEM((2, 8, 128), F32),
            pltpu.VMEM((PLANE, 2, 8, 128), F32),
            pltpu.VMEM((8, 128), F32),
            pltpu.VMEM((SLABS, 8, 128), F32),
            pltpu.VMEM((PLANE, 2, 1, 128), F32),
            pltpu.VMEM((PLANE, 16, WIDE), BF16),
            pltpu.VMEM((PLANE, 16, WIDE), BF16),
            dma((5,)),
            dma((3,)),
            dma((SUBS, PLANE)), dma((SUBS, PLANE)),
            dma((2, 6)), dma((2, 6)),
            dma((5, SUBS)), dma((6, SUBS)),
            dma((5, SUBS)), dma((6, SUBS)),
            dma((2, SUBS)), dma((2, SUBS)),
            dma((RING,)), dma((RING,)),
            dma((RING,)), dma((RING,)),
            dma((PLANE,)), dma((PLANE,)),
            dma((SLABS,)), dma((SLABS,)),
            dma((PLANE,)), dma((PLANE,)),
        ],
        compiler_params=pltpu.CompilerParams(
            collective_id=0, has_side_effects=True, vmem_limit_bytes=63 * 1024 * 1024
        ),
    )(gradient[0], left_stat[0], right_stat[0], left_root[0], right_root[0])
    update, left_new, right_new = pl.pallas_call(
        place_out,
        out_shape=shapes,
        in_specs=[hbm] * 3,
        out_specs=(hbm, hbm, hbm),
        scratch_shapes=[
            pltpu.VMEM((ROWS, 2 * PLANE * BLK), BF16),
            pltpu.VMEM((QUART, BLK), F32),
            pltpu.VMEM((QUART, BLK), F32),
            dma((2, 3)),
        ],
        compiler_params=pltpu.CompilerParams(vmem_limit_bytes=63 * 1024 * 1024),
    )(update, left_new, right_new)
    return (update[None], left_new[None], right_new[None])


def solution(mesh):
    spec = P("mp", "dp", None)
    return jax.shard_map(
        on_device, mesh=mesh, in_specs=(spec,) * 5, out_specs=(spec,) * 3, check_vma=False
    )
```

time: 358 us -> 78.3 us (0.22)
  blocking collectives: 119 us -> 0 us
  waiting for transfers between devices: 119 us -> 0 us
  starting transfers between devices: 89.4 us -> 0 us
  Pallas kernels: 0 us -> 77.5 us
  local copies, waits for them, and re-layouts: 9.99 us -> 0 us
  other arithmetic: 9.69 us -> 0 us
  matrix products: 5.37 us -> 0 us
  between operations: 4.72 us -> 0.64 us
    ppermute x20 -> x0, waiting for transfers between devices: 119 us -> none  [swapped(): return lax.ppermute(value, axis, pairs)]
    psum x1 -> x0, blocking collectives: 119 us -> none  [on_device(): total = lax.psum(jnp.sum(jnp.square(grafted)), ('dp', 'mp')) / numel]
    ppermute x20 -> x0, starting transfers between devices: 89.4 us -> none  [swapped(): return lax.ppermute(value, axis, pairs)]
    pallas_call x0 -> x2, Pallas kernels: none -> 77.5 us  [the longest x1 75.3 us: on_device(): pl.pallas_call(kernel, out_shape=shapes, in_specs=[hbm] * 5, out_specs=(h...]
    another operation x25 -> x0, local copies, waits for them, and re-layouts: 6.31 us -> none  [the longest x1 1.47 us: on_device(): outbound = flat_rows.reshape(row_count, dp_count, COLS).transpose(1, 0, 2)]
    dot_general x3 -> x0, matrix products: 5.37 us -> none  [the longest x1 2.5 us: on_device(): precond = jnp.dot(lroot_full, mixed, preferred_element_type=jnp.float32)]
    select_n x20 -> x0, other arithmetic: 4.27 us -> none  [the longest x2 1.73 us: butterfly(): keep_half = jnp.where(upper_side, upper_half, lower_half)]
  transfers between devices with their start and end apart: 20 -> 0, of which waited for: 18 -> 0; matrix products, arithmetic and copies ran while one was open for 2% -> 0% of each run, Pallas kernels for 0% -> 0%
where the time goes in v1:
time: 78.3 us; the launch traced here: 78.2 us
  Pallas kernels  77.5 us (99%)
    pallas_call x1, Pallas kernels, on_device(): pl.pallas_call(kernel, out_shape=shapes, in_specs=[hbm] * 5, out_specs=(h...  75.3 us
    pallas_call x1, Pallas kernels, on_device(): pl.pallas_call(place_out, out_shape=shapes, in_specs=[hbm] * 3, out_specs...  2.25 us

profile of v1, /device:TPU:1, one launch (start us, length us, event | category | flops | bytes accessed | tf_op | source)
XLA Modules:
  0.0 78.2 jit_solution(10353461613171439777)
XLA Ops:
  0.6 75.3 %shard_map.76 = (bf16[6,24576]{1,0:T(8,128)(2,1)}, f32[192,768]{1,0:T(8,128)}, f32[192,768]{1,0:T(8,128)}) custom-call(bf16[6,24576]{1,0:T(8,128)(2,1)} %bitcast.10, f32[192,768]{1,0:T(8,128)} %bitcast.8, f32[192,768]{1,0:T(8,128)} %bitcast.9, bf16[192,768]{1,0:T(8,128)(2,1)} %bitcast.11, bf16[192,768]{1,0:T(8,128)(2,1)} %bitcast.12), custom_call_target="tpu_custom_call" | custom-call | tf_op jit(solution)/shard_map/pallas_call | solution.py:438
  75.9 2.3 %shard_map.77 = (bf16[6,24576]{1,0:T(8,128)(2,1)}, f32[192,768]{1,0:T(8,128)}, f32[192,768]{1,0:T(8,128)}) custom-call(bf16[6,24576]{1,0:T(8,128)(2,1)} %get-tuple-element.9.upd, f32[192,768]{1,0:T(8,128)} %get-tuple-element.10.lnew, f32[192,768]{1,0:T(8,128)} %get-tuple-element.11.rnew), custom_call_target="tpu_custom_call" | custom-call | tf_op jit(solution)/shard_map/pallas_call | solution.py:492

commit v2 on v1

--- a/solution.py
+++ b/solution.py
@@ -287,7 +287,7 @@
         ring_s.append(cs)
     ubuf[...] = direction.astype(BF16).reshape(RING, 48, 384)
     ring_u = []
-    for off in (4, 3, 5, 2, 6, 1, 7):
+    for off in (4, 2, 6, 3, 5, 1, 7):
         t, where = ring_id(off)
         cu = remote(ubuf.at[t], recvu.at[y], su.at[off], ru.at[off], where)
         cu.start()
@@ -350,9 +350,15 @@
 
     place = one_hot(128, 96, spread)
     place_last = [one_hot(128, 96, spread_last(block)) for block in range(3)]
-    for cu in ring_u:
-        cu.wait_recv()
-    for e in range(2):
+    second = []
+    for off in range(1, PLANE):
+        t, where = plane_id(off)
+        second.append(remote(send2.at[t], recv2.at[p], s2.at[off], r2.at[off], where))
+
+    for group in range(2):
+        e = (parity + group) % 2
+        for cu in ring_u[:3] if group == 0 else ring_u[3:]:
+            cu.wait_recv()
         both = [jnp.concatenate([recvu[2 * k + e], recvu[4 + 2 * k + e]], axis=0) for k in range(2)]
         both = jnp.concatenate(both, axis=1)
         last = jnp.concatenate([dot(at, both[:, WIDE:]) for at in place_last], axis=1)
@@ -361,12 +367,15 @@
         for s in range(2):
             for xx in range(4):
                 send2[(e + 2 * s) * 4 + xx] = out[(4 * s + xx) * 16 : (4 * s + xx) * 16 + 16]
-    second = []
-    for off in range(1, PLANE):
-        t, where = plane_id(off)
-        cp = remote(send2.at[t], recv2.at[p], s2.at[off], r2.at[off], where)
-        cp.start()
-        second.append(cp)
+        z, x = p // 4, p % 4
+        for s in (1, 0):
+            for dx in (2, 1, 3, 0):
+                t = (z + (e + z) % 2 + 2 * s) % 4 * 4 + (x + dx) % 4
+                off = (t + PLANE - p) % PLANE
+
+                @pl.when(off > 0)
+                def _():
+                    remote(send2.at[t], recv2.at[p], s2.at[off], r2.at[off], (t * RING + y, mp)).start()
 
     for cp in plane_s:
         cp.wait_recv()

time: 78.3 us -> 78.4 us (level)
  no operation moved by 1% of the time
where the time goes in v2:
time: 78.4 us; the launch traced here: 78.2 us
  Pallas kernels  77.6 us (99%)
    pallas_call x1, Pallas kernels, on_device(): pl.pallas_call(kernel, out_shape=shapes, in_specs=[hbm] * 5, out_specs=(h...  75.3 us
    pallas_call x1, Pallas kernels, on_device(): pl.pallas_call(place_out, out_shape=shapes, in_specs=[hbm] * 3, out_specs...  2.25 us

profile of v2, /device:TPU:1, one launch (start us, length us, event | category | flops | bytes accessed | tf_op | source)
XLA Modules:
  0.0 78.2 jit_solution(8060029115599293607)
XLA Ops:
  0.6 75.3 %shard_map.76 = (bf16[6,24576]{1,0:T(8,128)(2,1)}, f32[192,768]{1,0:T(8,128)}, f32[192,768]{1,0:T(8,128)}) custom-call(bf16[6,24576]{1,0:T(8,128)(2,1)} %bitcast.10, f32[192,768]{1,0:T(8,128)} %bitcast.8, f32[192,768]{1,0:T(8,128)} %bitcast.9, bf16[192,768]{1,0:T(8,128)(2,1)} %bitcast.11, bf16[192,768]{1,0:T(8,128)(2,1)} %bitcast.12), custom_call_target="tpu_custom_call" | custom-call | tf_op jit(solution)/shard_map/pallas_call | solution.py:447
  76.0 2.3 %shard_map.77 = (bf16[6,24576]{1,0:T(8,128)(2,1)}, f32[192,768]{1,0:T(8,128)}, f32[192,768]{1,0:T(8,128)}) custom-call(bf16[6,24576]{1,0:T(8,128)(2,1)} %get-tuple-element.9.upd, f32[192,768]{1,0:T(8,128)} %get-tuple-element.10.lnew, f32[192,768]{1,0:T(8,128)} %get-tuple-element.11.rnew), custom_call_target="tpu_custom_call" | custom-call | tf_op jit(solution)/shard_map/pallas_call | solution.py:501

commit v3 on v2

--- a/solution.py
+++ b/solution.py
@@ -17,6 +17,7 @@
 SLABS = 6
 ROWS = 6
 QUART = 192
+PARTS = 4
 WIDE = 640
 SUBS = 2
 CHUNK = PLANE * ROWS
@@ -48,11 +49,20 @@
     return lax.dot_general(a, b, (((1,), (1,)), ((), ())), preferred_element_type=F32)
 
 
+def column_part(i):
+    size = 2 * PLANE * BLK // PARTS
+    return pl.ds(i * size, size)
+
+
+def row_part(i):
+    return pl.ds(i * (QUART // PARTS), QUART // PARTS)
+
+
 def kernel(
     grad, lstat, rstat, lroot, rroot, upd_out, lnew_out, rnew_out,
     upd, lnew, rnew, gin, lold, rold, gsend, recv1, gfull, obuf, tbuf, rrp, lrp, order, cols, leftp, leftq, mixed, gsq, gtrue, ubuf, recvu,
     stat, recvs, msg, recvp, tot, recvt, coef, send2, recv2,
-    sload, sstore, s1, r1, sx, rx, sr, rr, sl, rl, st, rt, su, ru, ss, rs, sp, rp, sm, rm, s2, r2,
+    sload, sgrad, sstore, s1, r1, sx, rx, sr, rr, sl, rl, st, rt, su, ru, ss, rs, sp, rp, sm, rm, s2, r2,
 ):
     me = lax.axis_index("dp")
     mp = lax.axis_index("mp")
@@ -82,10 +92,16 @@
     loads = [
         pltpu.make_async_copy(src, dst, sload.at[i])
         for i, (src, dst) in enumerate(
-            ((grad, gin), (rroot, rrp.at[parity]), (lroot, lrp.at[upper]), (lstat, lold), (rstat, rold))
+            ((None, None), (rroot, rrp.at[parity]), (lroot, lrp.at[upper]), (lstat, lold), (rstat, rold))
         )
+        if i
     ]
-    loads[0].start()
+    loads = [None] + loads
+    pieces = [
+        pltpu.make_async_copy(grad.at[:, column_part(i)], gin.at[:, column_part(i)], sgrad.at[i]) for i in range(PARTS)
+    ]
+    for cp in pieces:
+        cp.start()
     barrier = pltpu.get_barrier_semaphore()
     peers = [plane_id(o)[1] for o in range(1, PLANE)]
     peers += [ring_id(o)[1] for o in range(1, RING)]
@@ -125,7 +141,8 @@
         mine = ref[slot, pl.ds(pl.multiple_of(own * 128 - lane * QUART, 64), 128), :]
         ref[1 - slot, :, lanes128(own)] = dot_nt(pick.astype(BF16), mine).astype(BF16)
 
-    loads[0].wait()
+    for cp in pieces:
+        cp.wait()
     first = []
     for sub in range(SUBS):
         for q in range(PLANE):
@@ -414,8 +431,11 @@
     for off in range(1, PLANE):
         second[off - 1].wait_recv()
         finish((p + PLANE - off) % PLANE)
-    stores.append(pltpu.make_async_copy(upd, upd_out, sstore.at[2]))
-    stores[2].start()
+    for i in range(PARTS):
+        stores.append(
+            pltpu.make_async_copy(upd.at[:, column_part(i)], upd_out.at[:, column_part(i)], sstore.at[2 + i])
+        )
+        stores[2 + i].start()
 
     for cp in second + mp_s:
         cp.wait_send()
@@ -424,7 +444,12 @@
 
 
 def place_out(upd, lnew, rnew, upd_out, lnew_out, rnew_out, upd_mid, lnew_mid, rnew_mid, sem):
-    legs = ((lnew, lnew_mid, lnew_out), (rnew, rnew_mid, rnew_out), (upd, upd_mid, upd_out))
+    legs = []
+    for i in range(PARTS):
+        r, c = row_part(i), column_part(i)
+        legs.append((lnew.at[r], lnew_mid.at[r], lnew_out.at[r]))
+        legs.append((rnew.at[r], rnew_mid.at[r], rnew_out.at[r]))
+        legs.append((upd.at[:, c], upd_mid.at[:, c], upd_out.at[:, c]))
     inward = [pltpu.make_async_copy(a, b, sem.at[0, i]) for i, (a, b, _) in enumerate(legs)]
     outward = [pltpu.make_async_copy(b, c, sem.at[1, i]) for i, (_, b, c) in enumerate(legs)]
     for cp in inward:
@@ -482,7 +507,8 @@
             pltpu.VMEM((PLANE, 16, WIDE), BF16),
             pltpu.VMEM((PLANE, 16, WIDE), BF16),
             dma((5,)),
-            dma((3,)),
+            dma((PARTS,)),
+            dma((2 + PARTS,)),
             dma((SUBS, PLANE)), dma((SUBS, PLANE)),
             dma((2, 6)), dma((2, 6)),
             dma((5, SUBS)), dma((6, SUBS)),
@@ -507,7 +533,7 @@
             pltpu.VMEM((ROWS, 2 * PLANE * BLK), BF16),
             pltpu.VMEM((QUART, BLK), F32),
             pltpu.VMEM((QUART, BLK), F32),
-            dma((2, 3)),
+            dma((2, 3 * PARTS)),
         ],
         compiler_params=pltpu.CompilerParams(vmem_limit_bytes=63 * 1024 * 1024),
     )(update, left_new, right_new)

time: 78.4 us -> 78.5 us (level)
  no operation moved by 1% of the time
where the time goes in v3:
time: 78.5 us; the launch traced here: 78.4 us
  Pallas kernels  77.7 us (99%)
    pallas_call x1, Pallas kernels, on_device(): pl.pallas_call(kernel, out_shape=shapes, in_specs=[hbm] * 5, out_specs=(h...  75.4 us
    pallas_call x1, Pallas kernels, on_device(): pl.pallas_call(place_out, out_shape=shapes, in_specs=[hbm] * 3, out_specs...  2.34 us

profile of v3, /device:TPU:1, one launch (start us, length us, event | category | flops | bytes accessed | tf_op | source)
XLA Modules:
  0.0 78.4 jit_solution(15726313490694155956)
XLA Ops:
  0.6 75.4 %shard_map.76 = (bf16[6,24576]{1,0:T(8,128)(2,1)}, f32[192,768]{1,0:T(8,128)}, f32[192,768]{1,0:T(8,128)}) custom-call(bf16[6,24576]{1,0:T(8,128)(2,1)} %bitcast.10, f32[192,768]{1,0:T(8,128)} %bitcast.8, f32[192,768]{1,0:T(8,128)} %bitcast.9, bf16[192,768]{1,0:T(8,128)(2,1)} %bitcast.11, bf16[192,768]{1,0:T(8,128)(2,1)} %bitcast.12), custom_call_target="tpu_custom_call" | custom-call | tf_op jit(solution)/shard_map/pallas_call | solution.py:472
  76.0 2.3 %shard_map.77 = (bf16[6,24576]{1,0:T(8,128)(2,1)}, f32[192,768]{1,0:T(8,128)}, f32[192,768]{1,0:T(8,128)}) custom-call(bf16[6,24576]{1,0:T(8,128)(2,1)} %get-tuple-element.9.upd, f32[192,768]{1,0:T(8,128)} %get-tuple-element.10.lnew, f32[192,768]{1,0:T(8,128)} %get-tuple-element.11.rnew), custom_call_target="tpu_custom_call" | custom-call | tf_op jit(solution)/shard_map/pallas_call | solution.py:527

commit v4 on v2

--- a/solution.py
+++ b/solution.py
@@ -116,8 +116,6 @@
         return copies
 
     shift_r, shift_l = 1 - 2 * parity, 2 - 4 * upper
-    xr = root_copies(0, rroot, rrp, parity, shift_r)
-    xl = root_copies(1, lroot, lrp, upper, shift_l)
 
     def fill(ref, slot, shift):
         own = outside(lane)
@@ -139,6 +137,9 @@
             cp.start()
             copies.append(cp)
         first.append(copies)
+        if sub == 0:
+            xr = root_copies(0, rroot, rrp, parity, shift_r)
+            xl = root_copies(1, lroot, lrp, upper, shift_l)
         recv1[sub, p] = gsend[sub, p]
 
     def compact(c):

time: 78.4 us -> 78.5 us (level)
  no operation moved by 1% of the time
where the time goes in v4:
time: 78.5 us; the launch traced here: 78.3 us
  Pallas kernels  77.7 us (99%)
    pallas_call x1, Pallas kernels, on_device(): pl.pallas_call(kernel, out_shape=shapes, in_specs=[hbm] * 5, out_specs=(h...  75.4 us
    pallas_call x1, Pallas kernels, on_device(): pl.pallas_call(place_out, out_shape=shapes, in_specs=[hbm] * 3, out_specs...  2.25 us

profile of v4, /device:TPU:1, one launch (start us, length us, event | category | flops | bytes accessed | tf_op | source)
XLA Modules:
  0.0 78.3 jit_solution(17404692179796635434)
XLA Ops:
  0.6 75.4 %shard_map.76 = (bf16[6,24576]{1,0:T(8,128)(2,1)}, f32[192,768]{1,0:T(8,128)}, f32[192,768]{1,0:T(8,128)}) custom-call(bf16[6,24576]{1,0:T(8,128)(2,1)} %bitcast.10, f32[192,768]{1,0:T(8,128)} %bitcast.8, f32[192,768]{1,0:T(8,128)} %bitcast.9, bf16[192,768]{1,0:T(8,128)(2,1)} %bitcast.11, bf16[192,768]{1,0:T(8,128)(2,1)} %bitcast.12), custom_call_target="tpu_custom_call" | custom-call | tf_op jit(solution)/shard_map/pallas_call | solution.py:448
  76.0 2.3 %shard_map.77 = (bf16[6,24576]{1,0:T(8,128)(2,1)}, f32[192,768]{1,0:T(8,128)}, f32[192,768]{1,0:T(8,128)}) custom-call(bf16[6,24576]{1,0:T(8,128)(2,1)} %get-tuple-element.9.upd, f32[192,768]{1,0:T(8,128)} %get-tuple-element.10.lnew, f32[192,768]{1,0:T(8,128)} %get-tuple-element.11.rnew), custom_call_target="tpu_custom_call" | custom-call | tf_op jit(solution)/shard_map/pallas_call | solution.py:502
